TPU v7x, 256 devices: a whole 4x4x8 slice. The times are simulated.
256 devices in a mesh: dense: 2 (over core), tp: 8 (over z), attn: 16 (over x, y).
Axes of the slice: x: 4, y: 4, z: 8, core: 2. Of those that a mesh axis runs over, the one named last changes fastest.
Arguments:
- hidden: bfloat16 [128, 8192], P('dense', 'attn'), may hold values from -6 to 6
- w_query: bfloat16 [8192, 8192], P('attn', 'tp'), may hold values from -0.0625 to 0.0625
- w_key: bfloat16 [8192, 1024], P('attn', 'tp'), may hold values from -0.0625 to 0.0625
- w_value: bfloat16 [8192, 1024], P('attn', 'tp'), may hold values from -0.0625 to 0.0625
- b_query: bfloat16 [8192], P('tp'), may hold values from -3 to 3
- b_key: bfloat16 [1024], P('tp'), may hold values from -6 to 6
- b_value: bfloat16 [1024], P('tp'), may hold values from -6 to 6
- w_out: bfloat16 [8192, 8192], P('tp', 'attn'), may hold values from -0.0625 to 0.0625
- k_cache: bfloat16 [128, 4096, 1024], P(('dense', 'attn'), None, 'tp'), may hold values from -60 to 60
- value_cache: bfloat16 [128, 4096, 1024], P(('dense', 'attn'), None, 'tp'), may hold values from -6 to 6
- slot_seq: int32 [128], P(('dense', 'attn')), may hold values from 0 to 31, as said below
- slot_len: int32 [128], P(('dense', 'attn')), may hold values from 1 to 4096, as said below
Outputs:
- attn_out: bfloat16 [128, 8192], P('dense', 'attn')
Inputs may be any that keep to these rules, and one draw needn't show every extreme that they name: `slot_seq`: every transcript is named by one or more slots. `slot_len`: some slot holds exactly 4096 live tokens.
All inputs are finite; a program needn't handle non-finite values.
Results may differ from a plain program's by a relative error of at most 0.012.
The roundings to bfloat16 on the way count: a program that leaves them out, or rounds other values in their place, can miss the bound.
Values may be sent and summed in bfloat16 or wider, within the bound.
A program may use at most 128 MiB of HBM per device.

v0:
```python
import jax
import jax.numpy as jnp
from jax import lax
from jax.sharding import PartitionSpec as P

H = 64
KEY_HEADS = 8
HEAD_SIZE = 128
STEPS = 4


NEG = -1e30


def joined(value, axis, join):
    pieces = jax.tree.map(lambda part: lax.all_gather(part, axis), value)
    head = jax.tree.map(lambda part: part[0], pieces)
    tail = jax.tree.map(lambda part: part[1:], pieces)
    so_far, _ = lax.scan(lambda so_far, section: (join(so_far, section), None), head, tail)
    return so_far


def combine_parts(first_part, second_part):
    top = jnp.maximum(first_part[0], second_part[0])
    left = jnp.exp(first_part[0] - top)
    right = jnp.exp(second_part[0] - top)
    total = left * first_part[1] + right * second_part[1]
    mixed = left[..., None] * first_part[2] + right[..., None] * second_part[2]
    return (top, total, mixed)


def new_part(query_part, key_part, value_part, scale):
    scores = (
        jnp.einsum("tsghd,tugd->tghsu", query_part, key_part, preferred_element_type=jnp.float32)
        * scale
    )
    steps = scores.shape[-1]
    causal = jnp.arange(steps)[:, None] >= jnp.arange(steps)[None, :]
    scores = jnp.where(causal, scores, NEG)
    new_top = jnp.max(scores, axis=-1)
    weights = jnp.exp(scores - new_top[..., None])
    new_total = jnp.sum(weights, axis=-1)
    new_mixed = jnp.einsum(
        "tghsu,tugd->tghsd",
        weights.astype(jnp.bfloat16),
        value_part,
        preferred_element_type=jnp.float32,
    )
    return (new_top, new_total, new_mixed)


def on_device(
    hidden,
    w_query,
    w_key,
    w_value,
    b_query,
    b_key,
    b_value,
    w_out,
    k_cache,
    value_cache,
    slot_seq,
    slot_len,
):
    group = H // KEY_HEADS
    scale = HEAD_SIZE ** (-0.5)
    q_cols = w_query.shape[1]
    kv_cols = w_key.shape[1]
    kv_heads = kv_cols // HEAD_SIZE
    capacity = k_cache.shape[1]
    partial_value = jnp.concatenate(
        [
            jnp.dot(hidden, w_query, preferred_element_type=jnp.float32),
            jnp.dot(hidden, w_key, preferred_element_type=jnp.float32),
            jnp.dot(hidden, w_value, preferred_element_type=jnp.float32),
        ],
        axis=1,
    )
    biases = jnp.concatenate([b_query, b_key, b_value]).astype(jnp.float32)
    summed = lax.psum(partial_value, "attn")
    own_rows = (summed + biases).astype(jnp.bfloat16)
    every_row = lax.all_gather(own_rows, "dense", axis=0, tiled=True)
    trans = every_row.shape[0] // STEPS
    query = every_row[:, :q_cols].reshape(trans, STEPS, kv_heads, group, HEAD_SIZE)
    new_key = every_row[:, q_cols : q_cols + kv_cols].reshape(trans, STEPS, kv_heads, HEAD_SIZE)
    new_value = every_row[:, q_cols + kv_cols :].reshape(trans, STEPS, kv_heads, HEAD_SIZE)

    def per_slot(items):
        keys, values, owner, live = items
        rows = lax.dynamic_index_in_dim(query, owner, 0, keepdims=False)
        keys = keys.reshape(capacity, kv_heads, HEAD_SIZE)
        values = values.reshape(capacity, kv_heads, HEAD_SIZE)
        scores = (
            jnp.einsum("sghd,cgd->ghsc", rows, keys, preferred_element_type=jnp.float32) * scale
        )
        valid = jnp.arange(capacity, dtype=jnp.int32) < live
        scores = jnp.where(valid, scores, NEG)
        top = jnp.max(scores, axis=-1)
        weights = jnp.exp(scores - top[..., None])
        total = jnp.sum(weights, axis=-1)
        mixed = jnp.einsum(
            "ghsc,cgd->ghsd",
            weights.astype(jnp.bfloat16),
            values,
            preferred_element_type=jnp.float32,
        )
        return (top, total, mixed)

    slot_top, slot_total, slot_mixed = lax.map(per_slot, (k_cache, value_cache, slot_seq, slot_len))
    onehot = slot_seq[:, None] == jnp.arange(trans, dtype=jnp.int32)[None, :]
    mask = onehot[:, :, None, None, None]
    local_top = jnp.max(jnp.where(mask, slot_top[:, None], NEG), axis=0)
    factor = jnp.exp(jnp.where(mask, slot_top[:, None] - local_top[None], NEG))
    local_total = jnp.sum(factor * slot_total[:, None], axis=0)
    local_mixed = jnp.einsum(
        "jtghs,jghsd->tghsd", factor, slot_mixed, precision=lax.Precision.HIGHEST
    )
    best, total, mixed = joined(
        (local_top, local_total, local_mixed), ("dense", "attn"), combine_parts
    )
    half = trans // lax.axis_size("dense")
    begin = lax.axis_index("dense") * half
    best = lax.dynamic_slice_in_dim(best, begin, half, 0)
    total = lax.dynamic_slice_in_dim(total, begin, half, 0)
    mixed = lax.dynamic_slice_in_dim(mixed, begin, half, 0)
    query_half = lax.dynamic_slice_in_dim(query, begin, half, 0)
    key_half = lax.dynamic_slice_in_dim(new_key, begin, half, 0)
    value_half = lax.dynamic_slice_in_dim(new_value, begin, half, 0)
    new_top, new_total, new_mixed = new_part(query_half, key_half, value_half, scale)
    final_top, final_total, final_mixed = combine_parts(
        (best, total, mixed), (new_top, new_total, new_mixed)
    )
    attention = final_mixed / final_total[..., None]
    attention = (
        jnp.transpose(attention, (0, 3, 1, 2, 4)).reshape(half * STEPS, q_cols).astype(jnp.bfloat16)
    )
    terms = jnp.dot(attention, w_out, preferred_element_type=jnp.float32)
    return lax.psum(terms, "tp").astype(jnp.bfloat16)


def solution(mesh):
    in_specs = (
        P("dense", "attn"),
        P("attn", "tp"),
        P("attn", "tp"),
        P("attn", "tp"),
        P("tp"),
        P("tp"),
        P("tp"),
        P("tp", "attn"),
        P(("dense", "attn"), None, "tp"),
        P(("dense", "attn"), None, "tp"),
        P(("dense", "attn")),
        P(("dense", "attn")),
    )
    out_specs = P("dense", "attn")
    return jax.shard_map(
        on_device, mesh=mesh, in_specs=in_specs, out_specs=out_specs, check_vma=False
    )
```

profile of v0, /device:TPU:8, one launch (start us, length us, event | category | flops | bytes accessed | tf_op | source)
XLA Modules:
  0.0 497.6 jit_solution(2279335270167837673)
XLA Ops:
  6.5 1.2 fusion.64
  7.7 1.1 fusion.65
  8.8 1.1 fusion.63
  12.3 94.7 %all-reduce.3.cloned.1.call-done = f32[64,1280]{1,0:T(8,128)} async-done(((f32[64,1280]{1,0:T(8,128)}), f32[64,1280]{1,0:T(8,128)}) %all-reduce.3.cloned.1.call-update) | async-done | bytes 327696 | tf_op jit(solution)/shard_map/psum | solution.py:81
  108.0 2.0 all_gather.21
  110.2 28.9 %while.28 = (s32[]{:T(128)}, f32[4,1,8,4]{2,3,1,0:T(4,128)S(1)}, f32[4,1,8,4]{2,3,1,0:T(4,128)S(1)}, f32[4,1,8,4,128]{4,2,3,1,0:T(8,128)S(1)}, s32[4]{0:T(128)S(...) while((s32[]{:T(128)}, f32[4,1,8,4]{2,3,1,0:T(4,128)S(1)}, ...), condition=%wide.region_4.5_spmd, body=%wide.region_1.4_spmd.sunk | while | flops 68030400 | bytes 3714631 | solution.py:110
  113.8 1.8 fusion.83
  115.8 1.6 fusion.85
  121.0 1.8 fusion.83
  123.0 1.6 fusion.85
  128.3 1.8 fusion.83
  130.3 1.6 fusion.85
  135.5 1.8 fusion.83
  137.5 1.6 fusion.85
  139.3 1.9 convolution_bitcast_fusion.1
  141.6 91.9 %all-gather.1 = f32[1024,8,4]{1,2,0:T(4,128)S(1)} all-gather(f32[32,8,4]{1,2,0:T(4,128)S(1)} %copy.71), channel_id=3, replica_groups=mesh['dense'=2,'tp'=8,'attn'=16] {'dense','attn'}, dimensions={0}, use_global_device_ids=true | all-gather | bytes 135168 | tf_op jit(solution)/shard_map/all_gather | solution.py:16
  235.2 2.0 copy.81
  237.1 79.2 %all-gather = f32[1024,8,4]{1,2,0:T(4,128)S(1)} all-gather(f32[32,8,4]{1,2,0:T(4,128)S(1)} %copy.70), channel_id=2, replica_groups=mesh['dense'=2,'tp'=8,'attn'=16] {'dense','attn'}, dimensions={0}, use_global_device_ids=true | all-gather | bytes 135168 | tf_op jit(solution)/shard_map/all_gather | solution.py:16
  316.6 2.0 copy.80
  318.5 1.6 fusion.62
  320.3 1.1 slice.45
  321.8 11.2 %slice.48 = f32[992,1,8,4,128]{4,0,3,2,1:T(8,128)} slice(f32[1024,1,8,4,128]{4,0,3,2,1:T(8,128)} %all-gather.5.cloned.1.call-done), slice={[32:1024], [0:1], [0:8], [0:4], [0:128]} | slice | bytes 32505856 | tf_op jit(solution)/shard_map/slice | solution.py:18
  333.0 123.4 %while.29 = (s32[]{:T(128)}, f32[32,1,8,4]{0,3,2,1:T(4,128)S(1)}, f32[32,1,8,4]{0,3,2,1:T(4,128)S(1)}, f32[32,1,8,4,128]{4,3,2,1,0:T(4,128)S(1)}, f32[31,32,1,8,...) while((s32[]{:T(128)}, f32[32,1,8,4]{0,3,2,1:T(4,128)S(1)}, ...), condition=%wide.region_8.9_spmd, body=%wide.region_7.8_spmd.sunk | while | flops 400386 | bytes 2699369 | solution.py:19
  334.8 1.1 constant_dynamic-slice_fusion.2
  335.9 1.1 fusion.88
  338.8 1.1 constant_dynamic-slice_fusion.2
  339.8 1.1 fusion.88
  342.7 1.1 constant_dynamic-slice_fusion.2
  346.7 1.1 constant_dynamic-slice_fusion.2
  347.8 1.1 fusion.88
  350.7 1.1 constant_dynamic-slice_fusion.2
  351.8 1.1 fusion.88
  354.7 1.1 constant_dynamic-slice_fusion.2
  358.7 1.1 constant_dynamic-slice_fusion.2
  359.8 1.1 fusion.88
  362.6 1.1 constant_dynamic-slice_fusion.2
  363.7 1.1 fusion.88
  366.6 1.1 constant_dynamic-slice_fusion.2
  370.6 1.1 constant_dynamic-slice_fusion.2
  371.7 1.1 fusion.88
  374.6 1.1 constant_dynamic-slice_fusion.2
  378.6 1.1 constant_dynamic-slice_fusion.2
  379.7 1.1 fusion.88
  382.5 1.1 constant_dynamic-slice_fusion.2
  386.5 1.1 constant_dynamic-slice_fusion.2
  390.5 1.1 constant_dynamic-slice_fusion.2
  394.5 1.1 constant_dynamic-slice_fusion.2
  398.5 1.1 constant_dynamic-slice_fusion.2
  402.4 1.1 constant_dynamic-slice_fusion.2
  406.4 1.1 constant_dynamic-slice_fusion.2
  410.4 1.1 constant_dynamic-slice_fusion.2
  414.4 1.1 constant_dynamic-slice_fusion.2
  418.4 1.1 constant_dynamic-slice_fusion.2
  422.4 1.1 constant_dynamic-slice_fusion.2
  426.3 1.1 constant_dynamic-slice_fusion.2
  430.3 1.1 constant_dynamic-slice_fusion.2
  434.3 1.1 constant_dynamic-slice_fusion.2
  438.3 1.1 constant_dynamic-slice_fusion.2
  442.3 1.1 constant_dynamic-slice_fusion.2
  446.2 1.1 constant_dynamic-slice_fusion.2
  450.2 1.1 constant_dynamic-slice_fusion.2
  454.2 1.1 constant_dynamic-slice_fusion.2
  457.4 1.3 fusion.26
  459.1 31.6 %all-reduce.4 = bf16[64,512]{1,0:T(8,128)(2,1)} all-reduce(f32[64,512]{1,0:T(8,128)S(1)} %fusion.29), channel_id=1, replica_groups=mesh['dense'=2,'tp'=8,'attn'=16] {'tp'}, use_global_device_ids=true, to_apply=%region_11.12 | all-reduce | flops 32768 | bytes 196608 | tf_op jit(solution)/shard_map/psum | solution.py:139
  (243 shorter events, 96.3 us)
Async XLA Ops:
  6.5 2.3 copy-start
  6.5 103.6 %copy-start.4 = (s32[4]{0:T(128)S(1)}, s32[4]{0:T(128)}, u32[]{:S(2)}) copy-start(s32[4]{0:T(128)} %param.26) | copy-start | bytes 52
  6.5 103.6 %copy-start.3 = (s32[4]{0:T(128)S(1)}, s32[4]{0:T(128)}, u32[]{:S(2)}) copy-start(s32[4]{0:T(128)} %param.27) | copy-start | bytes 52
  6.5 100.5 %all-reduce.3.cloned.1.call-start = ((), (), s32[]{:S(2)}) async-start(), calls=%async_computation | async-start | bytes 655360 | tf_op jit(solution)/shard_map/psum | solution.py:81
  10.8 309.6 %all-gather.5.cloned.1.call-start = ((), (), s32[]{:S(2)}) async-start(), calls=%async_computation.1 | async-start | bytes 17301504 | tf_op jit(solution)/shard_map/all_gather | solution.py:16
  139.1 2.5 copy-start.2
  456.4 2.4 copy-start.1
Sparse Core Ops, SparseCore 0:
  10.9 96.1 all-reduce.2
  141.4 86.9 all-gather.4
where the time goes:
time: 507 us; the launch traced here: 498 us
  blocking collectives  205 us (40%)
  waiting for transfers between devices  94.8 us (19%)
  other arithmetic  86.9 us (17%)
  local copies, waits for them, and re-layouts  67.5 us (13%)
  matrix products  21.8 us (4%)
  between operations  13.6 us (3%)
  loops' own time  8.08 us (2%)
    all_gather x2, blocking collectives, joined(): pieces = jax.tree.map(lambda part: lax.all_gather(part, axis), value)  171 us
    psum x1, waiting for transfers between devices, on_device(): summed = lax.psum(partial_value, 'attn')  94.7 us
    mul x63, other arithmetic, combine_parts(): mixed = left[..., None] * first_part[2] + right[..., None] * second_part[2]  46.7 us
    dynamic_slice x31, local copies, waits for them, and re-layouts, joined(): lax.scan(lambda so_far, section: (join(so_far, section), None), head, tail)  33.8 us
    add x31, other arithmetic, combine_parts(): mixed = left[..., None] * first_part[2] + right[..., None] * second_part[2]  32.8 us
    psum x1, blocking collectives, on_device(): return lax.psum(terms, 'tp').astype(jnp.bfloat16)  31.6 us
    slice x3, local copies, waits for them, and re-layouts, joined(): tail = jax.tree.map(lambda part: part[1:], pieces)  11.5 us
  transfers between devices with their start and end apart: 2, of which 1 were waited for; matrix products, arithmetic and copies ran while one was open for 2% of the time, Pallas kernels for 0%

commit v1 on v0

v1 whole, which is shorter than its diff:
```python
import jax
import jax.numpy as jnp
from jax import lax
from jax.experimental import pallas as pl
from jax.experimental.pallas import tpu as pltpu
from jax.sharding import PartitionSpec as P

MESH = pl.DeviceIdType.MESH
F32 = jnp.float32
BF16 = jnp.bfloat16

STEPS = 4
GROUP = 8
E = 128
ROWS = STEPS * GROUP
PART = STEPS * (GROUP + 2)
TOKENS = 4096
CHUNK = 1024
SLOTS = 4
NA = 16
NZ = 8
NEG = -1e30
SCALE = E**-0.5 * 1.4426950408889634
FAR = sorted(
    range(1, NA), key=lambda k: -(min(k // 4, 4 - k // 4) + min(k % 4, 4 - k % 4))
)
FAR_Z = sorted(range(1, NZ), key=lambda k: -min(k, 8 - k))


def kernel(
    h_hbm, wq_hbm, wk_hbm, wv_hbm, bq_hbm, bk_hbm, bv_hbm, wo_hbm, kc_hbm, vc_hbm, seq, live,
    out,
    h, wq, wk, wv, bq, bk, bv, wo, kb, vb,
    parts, parts_in, total, q_all, scores, slot_o, slot_ml, seq_in, messages, mixed_out, mixed_in,
    att, att_wide, terms, terms_in, done,
    load_sem, s1, r1, s2, r2, s2f, r2f, ss, rs, sq, rq, s3, r3, s4, r4, s5, r5, s6, r6,
):
    d, z, a = lax.axis_index("dense"), lax.axis_index("tp"), lax.axis_index("attn")
    x, y = a // 4, a % 4
    sibling = (1 - d, z, a)

    def at(k):
        return ((x + k // 4) % 4) * 4 + (y + k % 4) % 4

    def before(k):
        return ((x + 4 - k // 4) % 4) * 4 + (y + 4 - k % 4) % 4

    barrier = pltpu.get_barrier_semaphore()
    for k in FAR:
        pl.semaphore_signal(barrier, inc=1, device_id=(d, z, at(k)), device_id_type=MESH)
    for k in FAR_Z:
        pl.semaphore_signal(barrier, inc=1, device_id=(d, (z + k) % NZ, a), device_id_type=MESH)
    pl.semaphore_signal(barrier, inc=1, device_id=sibling, device_id_type=MESH)

    first = [
        pltpu.make_async_copy(src, dst, load_sem.at[i])
        for i, (src, dst) in enumerate(
            [(h_hbm, h), (wq_hbm, wq), (wk_hbm, wk), (wv_hbm, wv), (bq_hbm, bq), (bk_hbm, bk), (bv_hbm, bv)]
        )
    ]
    later = [
        pltpu.make_async_copy(src, dst, load_sem.at[7 + i])
        for i, (src, dst) in enumerate([(kc_hbm, kb), (vc_hbm, vb), (wo_hbm, wo)])
    ]
    for copy in first:
        copy.start()
    for copy in first:
        copy.wait()
    for copy in later:
        copy.start()

    rows = h[...]
    for c in range(0, GROUP, 2):
        pair = jnp.dot(rows, wq[:, c * E : (c + 2) * E], preferred_element_type=F32)
        parts[pl.ds(c, 64, stride=10), :] = pair[:, :E]
        parts[pl.ds(c + 1, 64, stride=10), :] = pair[:, E:]
    parts[pl.ds(8, 64, stride=10), :] = jnp.dot(rows, wk[...], preferred_element_type=F32)
    parts[pl.ds(9, 64, stride=10), :] = jnp.dot(rows, wv[...], preferred_element_type=F32)

    def block(t):
        return pl.ds(pl.multiple_of(t * PART, PART), PART)

    pl.semaphore_wait(barrier, NA - 1 + NZ - 1 + 1)
    copies1 = [
        pltpu.make_async_remote_copy(
            parts.at[block(at(k))], parts_in.at[k], s1.at[k], r1.at[k], device_id=(d, z, at(k)), device_id_type=MESH
        )
        for k in FAR
    ]
    for copy in copies1:
        copy.start()
    seq_copy = pltpu.make_async_remote_copy(
        seq, seq_in, sq, rq, device_id=sibling, device_id_type=MESH
    )
    seq_copy.start()

    for c in range(GROUP):
        total[pl.ds(c, STEPS, stride=10), :] = jnp.broadcast_to(bq[pl.ds(c * E, E)].astype(F32)[None, :], (STEPS, E))
    total[pl.ds(8, STEPS, stride=10), :] = jnp.broadcast_to(bk[...].astype(F32)[None, :], (STEPS, E))
    total[pl.ds(9, STEPS, stride=10), :] = jnp.broadcast_to(bv[...].astype(F32)[None, :], (STEPS, E))
    so_far = parts[block(a), :]
    for copy, k in reversed(list(zip(copies1, FAR))):
        copy.wait_recv()
        so_far = so_far + parts_in[k]
    total[...] = total[...] + so_far
    own = d * NA + a
    for s in range(STEPS):
        scores[s * GROUP : (s + 1) * GROUP, :E] = total[s * 10 : s * 10 + GROUP, :]
    query = scores[:ROWS, :E].astype(BF16)
    q_all[own] = query

    copies2 = [
        pltpu.make_async_remote_copy(
            q_all.at[own], q_all.at[own], s2.at[k], r2.at[k], device_id=(d, z, at(k)), device_id_type=MESH
        )
        for k in FAR
    ]
    for copy in copies2:
        copy.start()

    def forward(k):
        t = d * NA + before(k)
        return pltpu.make_async_remote_copy(
            q_all.at[t], q_all.at[t], s2f.at[k], r2f.at[k], device_id=sibling, device_id_type=MESH
        )

    forwards = [forward(k) for k in range(NA)]
    forwards[0].start()

    wide = query.astype(F32)
    new_key = total[pl.ds(8, STEPS, stride=10), :].astype(BF16).astype(F32)
    new_value = total[pl.ds(9, STEPS, stride=10), :].astype(BF16).astype(F32)
    step_of = lax.broadcasted_iota(jnp.int32, (ROWS, 1), 0) // GROUP
    fresh = [
        jnp.where(step_of >= u, jnp.sum(wide * new_key[u : u + 1, :], axis=1, keepdims=True) * SCALE, NEG)
        for u in range(STEPS)
    ]
    new_top = jnp.maximum(jnp.maximum(fresh[0], fresh[1]), jnp.maximum(fresh[2], fresh[3]))
    new_total = jnp.zeros((ROWS, 1), F32)
    new_mixed = jnp.zeros((ROWS, E), F32)
    for u in range(STEPS):
        weight = jnp.exp2(fresh[u] - new_top)
        new_total = new_total + weight
        new_mixed = new_mixed + weight.astype(BF16).astype(F32) * new_value[u : u + 1, :]

    for copy in copies1:
        copy.wait_send()
    seq_copy.wait()
    for copy, k in reversed(list(zip(copies2, FAR))):
        copy.wait_recv()
        forwards[k].start()
    for copy in later:
        copy.wait()
    for k in range(NA):
        forwards[k].wait_recv()

    row64 = lax.broadcasted_iota(jnp.int32, (2 * ROWS, 1), 0)
    lane = lax.broadcasted_iota(jnp.int32, (2 * ROWS, CHUNK), 1)
    slot_copies = []
    for p in range(SLOTS // 2):
        i, j = 2 * p, 2 * p + 1
        qi, qj = q_all[seq[i]], q_all[seq[j]]
        none = jnp.zeros_like(qi)
        left = jnp.concatenate(
            [jnp.concatenate([qi, none], axis=1), jnp.concatenate([none, qj], axis=1)], axis=0
        )
        count = jnp.where(row64 < ROWS, live[i], live[j])
        top = jnp.full((2 * ROWS, E), NEG, F32)
        for c in range(0, TOKENS, CHUNK):
            keys = jnp.concatenate([kb[i, c : c + CHUNK, :], kb[j, c : c + CHUNK, :]], axis=1)
            sc = lax.dot_general(left, keys, (((1,), (1,)), ((), ())), preferred_element_type=F32)
            sc = jnp.where(lane < count - c, sc * SCALE, NEG)
            scores[:, c : c + CHUNK] = sc
            for e in range(0, CHUNK, E):
                top = jnp.maximum(top, sc[:, e : e + E])
        m = jnp.max(top, axis=1, keepdims=True)
        weight_sum = jnp.zeros((2 * ROWS, E), F32)
        mixed = jnp.zeros((2 * ROWS, 2 * E), F32)
        for c in range(0, TOKENS, CHUNK):
            weight = jnp.exp2(scores[:, c : c + CHUNK] - m)
            for e in range(0, CHUNK, E):
                weight_sum = weight_sum + weight[:, e : e + E]
            values = jnp.concatenate([vb[i, c : c + CHUNK, :], vb[j, c : c + CHUNK, :]], axis=1)
            mixed = mixed + jnp.dot(weight.astype(BF16), values, preferred_element_type=F32)
        l = jnp.sum(weight_sum, axis=1, keepdims=True)
        ml = jnp.where(lax.broadcasted_iota(jnp.int32, (2 * ROWS, E), 1) < E // 2, m, l)
        slot_o[p, 0], slot_o[p, 1] = mixed[:ROWS, :E], mixed[ROWS:, E:]
        slot_o[p, 2], slot_o[p, 3] = ml[:ROWS], ml[ROWS:]
        copy = pltpu.make_async_remote_copy(
            slot_o.at[p], slot_ml.at[p], ss.at[p], rs.at[p], device_id=sibling, device_id_type=MESH
        )
        copy.start()
        slot_copies.append(copy)

    for copy in copies2:
        copy.wait_send()
    for copy in forwards:
        copy.wait_send()
    for copy in slot_copies:
        copy.wait()

    owners = [seq[j] for j in range(SLOTS)] + [seq_in[j] for j in range(SLOTS)]
    where = [(slot_o, j) for j in range(SLOTS)] + [(slot_ml, j) for j in range(SLOTS)]
    tops, sums = [], []
    for ref, j in where:
        ml = ref[j // 2, 2 + j % 2]
        tops.append(jnp.broadcast_to(ml[:, :1], (ROWS, E)))
        sums.append(jnp.broadcast_to(ml[:, E // 2 : E // 2 + 1], (ROWS, E)))
    lane16 = lax.broadcasted_iota(jnp.int32, (16, E), 1)

    def tail(level):
        high = level.astype(BF16).astype(F32)
        middle = (level - high).astype(BF16).astype(F32)
        low = level - high - middle
        packed = jnp.zeros((16, E), F32)
        for n, piece in enumerate([high[:16], middle[:16], low[:16], high[16:], middle[16:], low[16:]]):
            packed = jnp.where(lane16 == n, piece, packed)
        return packed.astype(BF16)

    best = []
    for j in range(2 * SLOTS):
        m = tops[j]
        for i in range(2 * SLOTS):
            if i != j:
                m = jnp.maximum(m, jnp.where(owners[i] == owners[j], tops[i], NEG))
        best.append(m)
    factor = [jnp.exp2(tops[j] - best[j]) for j in range(2 * SLOTS)]
    scaled = [factor[j] * where[j][0][where[j][1] // 2, where[j][1] % 2] for j in range(2 * SLOTS)]
    sums = [factor[j] * sums[j] for j in range(2 * SLOTS)]
    for j in range(2 * SLOTS):
        o, l = scaled[j], sums[j]
        for i in range(2 * SLOTS):
            if i != j:
                same = owners[i] == owners[j]
                o = o + jnp.where(same, scaled[i], 0.0)
                l = l + jnp.where(same, sums[i], 0.0)
        messages[j, :ROWS, :] = (o / l).astype(BF16)
        messages[j, ROWS:, :] = tail(best[j] + jnp.log2(l))
    messages[2 * SLOTS, :ROWS, :] = jnp.zeros((ROWS, E), BF16)
    messages[2 * SLOTS, ROWS:, :] = tail(jnp.full((ROWS, E), NEG, F32))

    copies3 = []
    for k in FAR + [0]:
        t = d * NA + at(k)
        index = 2 * SLOTS
        for j in range(2 * SLOTS):
            index = jnp.where(owners[j] == t, j, index)
        if k == 0:
            mixed_in[0] = messages[index]
        else:
            mixed_out[k] = messages[index]
            copy = pltpu.make_async_remote_copy(
                mixed_out.at[k], mixed_in.at[k], s3.at[k], r3.at[k], device_id=(d, z, at(k)), device_id_type=MESH
            )
            copy.start()
            copies3.append(copy)
    for copy in reversed(copies3):
        copy.wait_recv()

    levels = []
    for k in range(NA):
        packed = mixed_in[k, ROWS:, :].astype(F32)
        upper = (packed[:, 0:1] + packed[:, 1:2]) + packed[:, 2:3]
        lower = (packed[:, 3:4] + packed[:, 4:5]) + packed[:, 5:6]
        levels.append(jnp.concatenate([upper, lower], axis=0))
    m = new_top
    for level in levels:
        m = jnp.maximum(m, level)
    weight = jnp.exp2(new_top - m)
    l = weight * new_total
    o = weight * new_mixed
    for k in range(NA):
        weight = jnp.exp2(levels[k] - m)
        l = l + weight
        o = o + weight * mixed_in[k, :ROWS, :].astype(F32)
    att[a] = (o / l).astype(BF16)

    copies4 = [
        pltpu.make_async_remote_copy(
            att.at[a], att.at[a], s4.at[k], r4.at[k], device_id=(d, z, at(k)), device_id_type=MESH
        )
        for k in FAR
    ]
    for copy in copies4:
        copy.start()
    for copy in copies3:
        copy.wait_send()
    for copy in reversed(copies4):
        copy.wait_recv()

    for t in range(NA):
        att_wide[t * ROWS : (t + 1) * ROWS, :] = att[t].astype(F32)
    result = jnp.zeros((64, 512), F32)
    for c in range(0, GROUP, 2):
        heads = jnp.concatenate(
            [
                att_wide[pl.ds(c, 64, stride=GROUP), :].astype(BF16),
                att_wide[pl.ds(c + 1, 64, stride=GROUP), :].astype(BF16),
            ],
            axis=1,
        )
        result = result + jnp.dot(heads, wo[c * E : (c + 2) * E, :], preferred_element_type=F32)
    for b in range(NZ):
        r, c = b % 4, b // 4
        terms[b] = result[r * 16 : (r + 1) * 16, c * 256 : (c + 1) * 256]
    copies5 = [
        pltpu.make_async_remote_copy(
            terms.at[(z + k) % NZ], terms_in.at[k], s5.at[k], r5.at[k],
            device_id=(d, (z + k) % NZ, a), device_id_type=MESH,
        )
        for k in FAR_Z
    ]
    for copy in copies5:
        copy.start()
    for copy in copies4:
        copy.wait_send()
    summed = terms[z]
    for copy, k in reversed(list(zip(copies5, FAR_Z))):
        copy.wait_recv()
        summed = summed + terms_in[k]
    done[...] = summed.astype(BF16)
    copies6 = [
        pltpu.make_async_remote_copy(
            done, out.at[z], s6.at[k], r6.at[k], device_id=(d, (z + k) % NZ, a), device_id_type=MESH
        )
        for k in FAR_Z
    ]
    for copy in copies6:
        copy.start()
    own_copy = pltpu.make_async_copy(done, out.at[z], load_sem.at[10])
    own_copy.start()
    for copy in copies5:
        copy.wait_send()
    own_copy.wait()
    for copy in copies6:
        copy.wait()


def on_device(*args):
    anywhere = pl.BlockSpec(memory_space=pl.ANY)
    scalars = pl.BlockSpec(memory_space=pltpu.SMEM)
    sems = pltpu.SemaphoreType.DMA
    blocks = pl.pallas_call(
        kernel,
        out_shape=jax.ShapeDtypeStruct((NZ, 16, 256), BF16),
        in_specs=[anywhere] * 10 + [scalars] * 2,
        out_specs=anywhere,
        scratch_shapes=[
            *(pltpu.VMEM(arg.shape, arg.dtype) for arg in args[:10]),
            pltpu.VMEM((NA * PART, E), F32),
            pltpu.VMEM((NA, PART, E), F32),
            pltpu.VMEM((PART, E), F32),
            pltpu.VMEM((2 * NA, ROWS, E), BF16),
            pltpu.VMEM((2 * ROWS, TOKENS), F32),
            pltpu.VMEM((2, 4, ROWS, E), F32),
            pltpu.VMEM((2, 4, ROWS, E), F32),
            pltpu.SMEM((SLOTS,), jnp.int32),
            pltpu.VMEM((2 * SLOTS + 1, ROWS + 16, E), BF16),
            pltpu.VMEM((NA, ROWS + 16, E), BF16),
            pltpu.VMEM((NA, ROWS + 16, E), BF16),
            pltpu.VMEM((NA, ROWS, E), BF16),
            pltpu.VMEM((NA * ROWS, E), F32),
            pltpu.VMEM((NZ, 16, 256), F32),
            pltpu.VMEM((NZ, 16, 256), F32),
            pltpu.VMEM((16, 256), BF16),
            sems((11,)),
            *[sems((NA,))] * 6,
            *[sems((2,))] * 2,
            sems(()),
            sems(()),
            *[sems((NA,))] * 4,
            *[sems((NZ,))] * 4,
        ],
        compiler_params=pltpu.CompilerParams(
            collective_id=0, has_side_effects=True, vmem_limit_bytes=56 << 20
        ),
        name="decode",
    )(*args)
    return blocks.reshape(2, 4, 16, 256).transpose(1, 2, 0, 3).reshape(64, 512)


def solution(mesh):
    in_specs = (
        P("dense", "attn"),
        P("attn", "tp"),
        P("attn", "tp"),
        P("attn", "tp"),
        P("tp"),
        P("tp"),
        P("tp"),
        P("tp", "attn"),
        P(("dense", "attn"), None, "tp"),
        P(("dense", "attn"), None, "tp"),
        P(("dense", "attn")),
        P(("dense", "attn")),
    )
    return jax.shard_map(
        on_device, mesh=mesh, in_specs=in_specs, out_specs=P("dense", "attn"), check_vma=False
    )
```

time: 507 us -> 50.1 us (0.10); the launches traced: 498 us -> 49.8 us
  blocking collectives: 205 us -> 0 us
  waiting for transfers between devices: 94.8 us -> 0 us
  other arithmetic: 86.9 us -> 0 us
  local copies, waits for them, and re-layouts: 67.5 us -> 1.55 us
  Pallas kernels: 0 us -> 48.2 us
  matrix products: 21.8 us -> 0 us
  between operations: 13.6 us -> 0.01 us
  loops' own time: 8.08 us -> 0 us
    all_gather x3 -> x0, blocking collectives: 173 us -> none  [the longest x2 171 us: joined(): pieces = jax.tree.map(lambda part: lax.all_gather(part, axis), value)]
    psum x1 -> x0, waiting for transfers between devices: 94.7 us -> none  [on_device(): summed = lax.psum(partial_value, 'attn')]
    pallas_call x0 -> x1, Pallas kernels: none -> 48.2 us  [on_device(): pl.pallas_call(kernel, out_shape=jax.ShapeDtypeStruct((NZ, 16, 256), BF16...]
    mul x63 -> x0, other arithmetic: 46.7 us -> none  [combine_parts(): mixed = left[..., None] * first_part[2] + right[..., None] * second_part[2]]
    dynamic_slice x39 -> x0, local copies, waits for them, and re-layouts: 38.8 us -> none  [the longest x31 33.8 us: joined(): lax.scan(lambda so_far, section: (join(so_far, section), None), head, tail)]
    add x31 -> x0, other arithmetic: 32.8 us -> none  [combine_parts(): mixed = left[..., None] * first_part[2] + right[..., None] * second_part[2]]
    psum x1 -> x0, blocking collectives: 31.6 us -> none  [on_device(): return lax.psum(terms, 'tp').astype(jnp.bfloat16)]
    dot_general x15 -> x0, matrix products: 21.8 us -> none  [the longest x4 7.04 us: per_slot(): jnp.einsum('sghd,cgd->ghsc', rows, keys, preferred_element_type=jnp.float32)]
  transfers between devices with their start and end apart: 2 -> 0, of which waited for: 1 -> 0; matrix products, arithmetic and copies ran while one was open for 2% -> 0% of each run, Pallas kernels for 0% -> 0%
where the time goes in v1:
time: 50.1 us; the launch traced here: 49.8 us
  Pallas kernels  48.2 us (96%)
  local copies, waits for them, and re-layouts  1.55 us (3%)
    pallas_call x1, Pallas kernels, on_device(): pl.pallas_call(kernel, out_shape=jax.ShapeDtypeStruct((NZ, 16, 256), BF16...  48.2 us

profile of v1, /device:TPU:8, one launch (start us, length us, event | category | flops | bytes accessed | tf_op | source)
XLA Modules:
  0.0 49.8 jit_solution(13197450042346756376)
XLA Ops:
  0.0 48.2 %decode.1 = bf16[8,16,256]{2,1,0:T(8,128)(2,1)} custom-call(bf16[64,512]{1,0:T(8,128)(2,1)} %h_hbm.1, bf16[512,1024]{1,0:T(8,128)(2,1)} %wq_hbm.1, bf16[512,128]{1,0:T(8,128)(2,1)} %wk_hbm.1, bf16[512,128]{1,0:T(8,128)(2,1)} %wv_hbm.1, bf16[1024]{0:T(1024)(128)(2,1)} %bq_hbm.1, bf16[128]{0:T(256)(128)(2,1)} %bk_hbm.1, bf16[128]{0:T(256)(128)(2,1)} %bv_hbm.1, ...), custom_call_target="tpu_custom_call" | custom-call | tf_op jit(solution)/shard_map/decode/pallas_call | solution.py:343
  48.3 0.9 %copy.13 = bf16[4,16,2,256]{3,2,1,0:T(2,128)(2,1)S(1)} copy(bf16[4,16,2,256]{3,1,0,2:T(8,128)(2,1)} %bitcast.6) | data formatting | bytes 131072 | tf_op jit(solution)/shard_map/transpose | solution.py:379
  49.2 0.6 %copy.14 = bf16[8,8,2,256]{3,1,2,0:T(8,128)(2,1)} copy(bf16[8,8,2,256]{3,2,1,0:T(2,128)(2,1)S(1)} %bitcast.7) | data formatting | bytes 131072

commit v2 on v1

v2 whole, which is shorter than its diff:
```python
import jax
import jax.numpy as jnp
from jax import lax
from jax.experimental import pallas as pl
from jax.experimental.pallas import tpu as pltpu
from jax.sharding import PartitionSpec as P

MESH = pl.DeviceIdType.MESH
F32 = jnp.float32
BF16 = jnp.bfloat16

STEPS = 4
GROUP = 8
E = 128
ROWS = STEPS * GROUP
STRIDE = GROUP + 2
PART = STEPS * STRIDE
TOKENS = 4096
CHUNK = 1024
SLOTS = 4
NA = 16
NZ = 8
NEG = -1e30
SCALE = E**-0.5 * 1.4426950408889634
FAR = [10, 6, 14, 9, 11, 5, 15, 7, 13, 2, 8, 1, 12, 3, 4]
FAR_Z = sorted(range(1, NZ), key=lambda k: -min(k, 8 - k))


def kernel(
    h_hbm, wq_hbm, wk_hbm, wv_hbm, bq_hbm, bk_hbm, bv_hbm, wo_hbm, kc_hbm, vc_hbm, seq_hbm, live_hbm,
    out,
    h, wq, wk, wv, bq, bk, bv, wo, kb, vb, seq, live,
    parts, parts_in, total, q_all, scores, slot_o, slot_in, seq_in, messages, mixed_out, mixed_in,
    att, att_wide, terms, terms_out, terms_in, done,
    load_sem, s1, r1, s2, r2, s2f, r2f, ss, rs, sq, rq, s3, r3, s4, r4, s5, r5, s6, r6,
):
    d, z, a = lax.axis_index("dense"), lax.axis_index("tp"), lax.axis_index("attn")
    x, y = a // 4, a % 4
    sibling = (1 - d, z, a)

    def at(k):
        return ((x + k // 4) % 4) * 4 + (y + k % 4) % 4

    def before(k):
        return ((x + 4 - k // 4) % 4) * 4 + (y + 4 - k % 4) % 4

    first = [
        pltpu.make_async_copy(src, dst, load_sem.at[i])
        for i, (src, dst) in enumerate(
            [(h_hbm, h), (wq_hbm, wq), (wk_hbm, wk), (wv_hbm, wv), (bq_hbm, bq), (bk_hbm, bk), (bv_hbm, bv)]
        )
    ]
    later = [
        pltpu.make_async_copy(src, dst, load_sem.at[7 + i])
        for i, (src, dst) in enumerate(
            [(seq_hbm, seq), (live_hbm, live), (kc_hbm, kb), (vc_hbm, vb), (wo_hbm, wo)]
        )
    ]
    for copy in first + later:
        copy.start()
    barrier = pltpu.get_barrier_semaphore()
    for k in FAR:
        pl.semaphore_signal(barrier, inc=1, device_id=(d, z, at(k)), device_id_type=MESH)
    for k in FAR:
        pl.semaphore_signal(barrier, inc=1, device_id=(1 - d, z, at(k)), device_id_type=MESH)
    for k in FAR_Z:
        pl.semaphore_signal(barrier, inc=1, device_id=(d, (z + k) % NZ, a), device_id_type=MESH)
    pl.semaphore_signal(barrier, inc=1, device_id=sibling, device_id_type=MESH)

    for copy in first:
        copy.wait()

    rows = h[...]
    for c in range(0, GROUP, 2):
        pair = jnp.dot(rows, wq[:, c * E : (c + 2) * E], preferred_element_type=F32)
        parts[pl.ds(c, 64, stride=STRIDE), :] = pair[:, :E]
        parts[pl.ds(c + 1, 64, stride=STRIDE), :] = pair[:, E:]
    parts[pl.ds(8, 64, stride=STRIDE), :] = jnp.dot(rows, wk[...], preferred_element_type=F32)
    parts[pl.ds(9, 64, stride=STRIDE), :] = jnp.dot(rows, wv[...], preferred_element_type=F32)

    def block(t):
        return pl.ds(pl.multiple_of(t * PART, PART), PART)

    pl.semaphore_wait(barrier, 2 * (NA - 1) + NZ - 1 + 1)
    copies1 = [
        pltpu.make_async_remote_copy(
            parts.at[block(at(k))], parts_in.at[k], s1.at[k], r1.at[k], device_id=(d, z, at(k)), device_id_type=MESH
        )
        for k in FAR
    ]
    for copy in copies1:
        copy.start()
    later[0].wait()
    seq_copy = pltpu.make_async_remote_copy(
        seq, seq_in, sq, rq, device_id=sibling, device_id_type=MESH
    )
    seq_copy.start()

    for c in range(GROUP):
        total[pl.ds(c, STEPS, stride=STRIDE), :] = jnp.broadcast_to(bq[pl.ds(c * E, E)].astype(F32)[None, :], (STEPS, E))
    total[pl.ds(8, STEPS, stride=STRIDE), :] = jnp.broadcast_to(bk[...].astype(F32)[None, :], (STEPS, E))
    total[pl.ds(9, STEPS, stride=STRIDE), :] = jnp.broadcast_to(bv[...].astype(F32)[None, :], (STEPS, E))
    so_far = parts[block(a), :]
    for copy, k in reversed(list(zip(copies1, FAR))):
        copy.wait_recv()
        so_far = so_far + parts_in[k]
    total[...] = total[...] + so_far
    own = d * NA + a
    for s in range(STEPS):
        scores[0, s * GROUP : (s + 1) * GROUP, :E] = total[s * STRIDE : s * STRIDE + GROUP, :]
    query = scores[0, :ROWS, :E].astype(BF16)
    q_all[own] = query

    copies2 = [
        pltpu.make_async_remote_copy(
            q_all.at[own], q_all.at[own], s2.at[k], r2.at[k], device_id=(d, z, at(k)), device_id_type=MESH
        )
        for k in FAR
    ]
    across = [
        pltpu.make_async_remote_copy(
            q_all.at[own], q_all.at[own], s2f.at[k], r2f.at[k], device_id=(1 - d, z, at(k)), device_id_type=MESH
        )
        for k in FAR
    ]
    for copy, other in zip(copies2, across):
        copy.start()
        other.start()
    across.append(
        pltpu.make_async_remote_copy(
            q_all.at[own], q_all.at[own], s2f.at[0], r2f.at[0], device_id=sibling, device_id_type=MESH
        )
    )
    across[-1].start()

    wide = query.astype(F32)
    new_key = total[pl.ds(8, STEPS, stride=STRIDE), :].astype(BF16).astype(F32)
    new_value = total[pl.ds(9, STEPS, stride=STRIDE), :].astype(BF16).astype(F32)
    step_of = lax.broadcasted_iota(jnp.int32, (ROWS, 1), 0) // GROUP
    fresh = [
        jnp.where(step_of >= u, jnp.sum(wide * new_key[u : u + 1, :], axis=1, keepdims=True) * SCALE, NEG)
        for u in range(STEPS)
    ]
    new_top = jnp.maximum(jnp.maximum(fresh[0], fresh[1]), jnp.maximum(fresh[2], fresh[3]))
    new_total = jnp.zeros((ROWS, 1), F32)
    new_mixed = jnp.zeros((ROWS, E), F32)
    for u in range(STEPS):
        weight = jnp.exp2(fresh[u] - new_top)
        new_total = new_total + weight
        new_mixed = new_mixed + weight.astype(BF16).astype(F32) * new_value[u : u + 1, :]

    for copy in copies1:
        copy.wait_send()
    seq_copy.wait()
    for copy in copies2:
        copy.wait_recv()
    for copy in later[1:]:
        copy.wait()
    for copy in across:
        copy.wait_recv()

    row64 = lax.broadcasted_iota(jnp.int32, (2 * ROWS, 1), 0)
    lane = lax.broadcasted_iota(jnp.int32, (2 * ROWS, CHUNK), 1)
    lane32 = lax.broadcasted_iota(jnp.int32, (ROWS, E), 1)
    ml = jnp.zeros((ROWS, E), F32)
    highest = []
    for p in range(SLOTS // 2):
        i, j = 2 * p, 2 * p + 1
        qi, qj = q_all[seq[i]], q_all[seq[j]]
        none = jnp.zeros_like(qi)
        left = jnp.concatenate(
            [jnp.concatenate([qi, none], axis=1), jnp.concatenate([none, qj], axis=1)], axis=0
        )
        count = jnp.where(row64 < ROWS, live[i], live[j])
        top = jnp.full((2 * ROWS, E), NEG, F32)
        for c in range(0, TOKENS, CHUNK):
            keys = jnp.concatenate([kb[i, c : c + CHUNK, :], kb[j, c : c + CHUNK, :]], axis=1)
            sc = lax.dot_general(left, keys, (((1,), (1,)), ((), ())), preferred_element_type=F32)
            sc = jnp.where(lane < count - c, sc * SCALE, NEG)
            scores[p, :, c : c + CHUNK] = sc
            for e in range(0, CHUNK, E):
                top = jnp.maximum(top, sc[:, e : e + E])
        highest.append(jnp.max(top, axis=1, keepdims=True))
    for p in range(SLOTS // 2):
        i, j, m = 2 * p, 2 * p + 1, highest[p]
        weight_sum = jnp.zeros((2 * ROWS, E), F32)
        mixed = jnp.zeros((2 * ROWS, 2 * E), F32)
        for c in range(0, TOKENS, CHUNK):
            weight = jnp.exp2(scores[p, :, c : c + CHUNK] - m)
            for e in range(0, CHUNK, E):
                weight_sum = weight_sum + weight[:, e : e + E]
            values = jnp.concatenate([vb[i, c : c + CHUNK, :], vb[j, c : c + CHUNK, :]], axis=1)
            mixed = mixed + jnp.dot(weight.astype(BF16), values, preferred_element_type=F32)
        l = jnp.sum(weight_sum, axis=1, keepdims=True)
        slot_o[i], slot_o[j] = mixed[:ROWS, :E], mixed[ROWS:, E:]
        for n, half in ((i, slice(ROWS)), (j, slice(ROWS, None))):
            ml = jnp.where(lane32 == n, m[half], ml)
            ml = jnp.where(lane32 == SLOTS + n, l[half], ml)
    slot_o[SLOTS] = ml
    slot_copy = pltpu.make_async_remote_copy(
        slot_o, slot_in, ss, rs, device_id=sibling, device_id_type=MESH
    )
    slot_copy.start()

    for copy in copies2:
        copy.wait_send()
    for copy in across:
        copy.wait_send()
    slot_copy.wait()

    owners = [seq[j] for j in range(SLOTS)] + [seq_in[j] for j in range(SLOTS)]
    where = [(slot_o, j) for j in range(SLOTS)] + [(slot_in, j) for j in range(SLOTS)]
    tops, sums = [], []
    for ref, j in where:
        ml = ref[SLOTS]
        tops.append(jnp.broadcast_to(ml[:, j : j + 1], (ROWS, E)))
        sums.append(jnp.broadcast_to(ml[:, SLOTS + j : SLOTS + j + 1], (ROWS, E)))
    lane16 = lax.broadcasted_iota(jnp.int32, (16, E), 1)

    def tail(level):
        high = level.astype(BF16).astype(F32)
        middle = (level - high).astype(BF16).astype(F32)
        low = level - high - middle
        packed = jnp.zeros((16, E), F32)
        for n, piece in enumerate([high[:16], middle[:16], low[:16], high[16:], middle[16:], low[16:]]):
            packed = jnp.where(lane16 == n, piece, packed)
        return packed.astype(BF16)

    best = []
    for j in range(2 * SLOTS):
        m = tops[j]
        for i in range(2 * SLOTS):
            if i != j:
                m = jnp.maximum(m, jnp.where(owners[i] == owners[j], tops[i], NEG))
        best.append(m)
    factor = [jnp.exp2(tops[j] - best[j]) for j in range(2 * SLOTS)]
    scaled = [factor[j] * where[j][0][where[j][1]] for j in range(2 * SLOTS)]
    sums = [factor[j] * sums[j] for j in range(2 * SLOTS)]
    for j in range(2 * SLOTS):
        o, l = scaled[j], sums[j]
        for i in range(2 * SLOTS):
            if i != j:
                same = owners[i] == owners[j]
                o = o + jnp.where(same, scaled[i], 0.0)
                l = l + jnp.where(same, sums[i], 0.0)
        messages[j, :ROWS, :] = (o / l).astype(BF16)
        messages[j, ROWS:, :] = tail(best[j] + jnp.log2(l))
    messages[2 * SLOTS, :ROWS, :] = jnp.zeros((ROWS, E), BF16)
    messages[2 * SLOTS, ROWS:, :] = tail(jnp.full((ROWS, E), NEG, F32))

    copies3 = []
    for k in FAR + [0]:
        t = d * NA + at(k)
        index = 2 * SLOTS
        for j in range(2 * SLOTS):
            index = jnp.where(owners[j] == t, j, index)
        if k == 0:
            mixed_in[0] = messages[index]
        else:
            mixed_out[k] = messages[index]
            copy = pltpu.make_async_remote_copy(
                mixed_out.at[k], mixed_in.at[k], s3.at[k], r3.at[k], device_id=(d, z, at(k)), device_id_type=MESH
            )
            copy.start()
            copies3.append(copy)
    for copy in reversed(copies3):
        copy.wait_recv()
    levels = []
    for k in range(NA):
        packed = mixed_in[k, ROWS:, :].astype(F32)
        upper = jnp.sum(jnp.where(lane16 < 3, packed, 0.0), axis=1, keepdims=True)
        lower = jnp.sum(jnp.where(lane16 < 3, 0.0, packed), axis=1, keepdims=True)
        levels.append(jnp.concatenate([upper, lower], axis=0))
    m = new_top
    for level in levels:
        m = jnp.maximum(m, level)
    weight = jnp.exp2(new_top - m)
    l = weight * new_total
    o = weight * new_mixed
    for k, level in enumerate(levels):
        weight = jnp.exp2(level - m)
        l = l + weight
        o = o + weight * mixed_in[k, :ROWS, :].astype(F32)
    att[a] = (o / l).astype(BF16)

    copies4 = [
        pltpu.make_async_remote_copy(
            att.at[a], att.at[a], s4.at[k], r4.at[k], device_id=(d, z, at(k)), device_id_type=MESH
        )
        for k in FAR
    ]
    for copy in copies4:
        copy.start()
    for copy in copies3:
        copy.wait_send()
    for n, k in enumerate([0] + FAR[::-1]):
        if k:
            copies4[NA - 1 - n].wait_recv()
        t = before(k)
        att_wide[pl.ds(pl.multiple_of(t * ROWS, ROWS), ROWS), :] = att[t].astype(F32)
    result = jnp.zeros((64, 512), F32)
    for c in range(0, GROUP, 2):
        heads = jnp.concatenate(
            [
                att_wide[pl.ds(c, 64, stride=GROUP), :].astype(BF16),
                att_wide[pl.ds(c + 1, 64, stride=GROUP), :].astype(BF16),
            ],
            axis=1,
        )
        result = result + jnp.dot(heads, wo[c * E : (c + 2) * E, :], preferred_element_type=F32)
    for b in range(NZ):
        r, c = b % 4, b // 4
        terms[b] = result[r * 16 : (r + 1) * 16, c * 256 : (c + 1) * 256]
        terms_out[b] = terms[b].astype(BF16)
    copies5 = [
        pltpu.make_async_remote_copy(
            terms_out.at[(z + k) % NZ], terms_in.at[k], s5.at[k], r5.at[k],
            device_id=(d, (z + k) % NZ, a), device_id_type=MESH,
        )
        for k in FAR_Z
    ]
    for copy in copies5:
        copy.start()
    for copy in copies4:
        copy.wait_send()
    summed = terms[z]
    for copy, k in reversed(list(zip(copies5, FAR_Z))):
        copy.wait_recv()
        summed = summed + terms_in[k].astype(F32)
    done[...] = summed.astype(BF16)
    place = out.at[pl.ds(pl.multiple_of(z % 4 * 16, 16), 16), pl.ds(pl.multiple_of(z // 4 * 256, 256), 256)]
    copies6 = [
        pltpu.make_async_remote_copy(
            done, place, s6.at[k], r6.at[k], device_id=(d, (z + k) % NZ, a), device_id_type=MESH
        )
        for k in FAR_Z
    ]
    for copy in copies6:
        copy.start()
    own_copy = pltpu.make_async_copy(done, place, load_sem.at[12])
    own_copy.start()
    for copy in copies5:
        copy.wait_send()
    own_copy.wait()
    for copy in copies6:
        copy.wait()


def on_device(*args):
    anywhere = pl.BlockSpec(memory_space=pl.ANY)
    sems = pltpu.SemaphoreType.DMA
    return pl.pallas_call(
        kernel,
        out_shape=pltpu.VMEM((64, 512), BF16),
        in_specs=[anywhere] * 12,
        out_specs=pl.BlockSpec(memory_space=pltpu.VMEM),
        scratch_shapes=[
            *(pltpu.VMEM(arg.shape, arg.dtype) for arg in args[:10]),
            *(pltpu.SMEM(arg.shape, arg.dtype) for arg in args[10:]),
            pltpu.VMEM((NA * PART, E), F32),
            pltpu.VMEM((NA, PART, E), F32),
            pltpu.VMEM((PART, E), F32),
            pltpu.VMEM((2 * NA, ROWS, E), BF16),
            pltpu.VMEM((2, 2 * ROWS, TOKENS), F32),
            pltpu.VMEM((SLOTS + 1, ROWS, E), F32),
            pltpu.VMEM((SLOTS + 1, ROWS, E), F32),
            pltpu.SMEM((SLOTS,), jnp.int32),
            pltpu.VMEM((2 * SLOTS + 1, ROWS + 16, E), BF16),
            pltpu.VMEM((NA, ROWS + 16, E), BF16),
            pltpu.VMEM((NA, ROWS + 16, E), BF16),
            pltpu.VMEM((NA, ROWS, E), BF16),
            pltpu.VMEM((NA * ROWS, E), F32),
            pltpu.VMEM((NZ, 16, 256), F32),
            pltpu.VMEM((NZ, 16, 256), BF16),
            pltpu.VMEM((NZ, 16, 256), BF16),
            pltpu.VMEM((16, 256), BF16),
            sems((13,)),
            *[sems((NA,))] * 6,
            *[sems(())] * 4,
            *[sems((NA,))] * 4,
            *[sems((NZ,))] * 4,
        ],
        compiler_params=pltpu.CompilerParams(
            collective_id=0, has_side_effects=True, vmem_limit_bytes=56 << 20
        ),
        name="decode",
    )(*args)


def solution(mesh):
    in_specs = (
        P("dense", "attn"),
        P("attn", "tp"),
        P("attn", "tp"),
        P("attn", "tp"),
        P("tp"),
        P("tp"),
        P("tp"),
        P("tp", "attn"),
        P(("dense", "attn"), None, "tp"),
        P(("dense", "attn"), None, "tp"),
        P(("dense", "attn")),
        P(("dense", "attn")),
    )
    return jax.shard_map(
        on_device, mesh=mesh, in_specs=in_specs, out_specs=P("dense", "attn"), check_vma=False
    )
```

time: 50.1 us -> 46.1 us (0.920)
  Pallas kernels: 48.2 us -> 45.3 us
  local copies, waits for them, and re-layouts: 1.55 us -> 0.63 us
    pallas_call x1, Pallas kernels: 48.2 us -> 45.3 us  [on_device(): pl.pallas_call(kernel, out_shape=pltpu.VMEM((64, 512), BF16), in_specs=[a...]
    transpose x1 -> x0, local copies, waits for them, and re-layouts: 0.91 us -> none  [on_device(): return blocks.reshape(2, 4, 16, 256).transpose(1, 2, 0, 3).reshape(64, 512)]
where the time goes in v2:
time: 46.1 us; the launch traced here: 45.9 us
  Pallas kernels  45.3 us (98%)
  local copies, waits for them, and re-layouts  0.63 us (1%)
    pallas_call x1, Pallas kernels, on_device(): pl.pallas_call(kernel, out_shape=pltpu.VMEM((64, 512), BF16), in_specs=[a...  45.3 us

profile of v2, /device:TPU:8, one launch (start us, length us, event | category | flops | bytes accessed | tf_op | source)
XLA Modules:
  0.0 45.9 jit_solution(4055322088008660135)
XLA Ops:
  0.0 45.3 %decode.1 = bf16[64,512]{1,0:T(8,128)(2,1)S(1)} custom-call(bf16[64,512]{1,0:T(8,128)(2,1)} %h_hbm.1, bf16[512,1024]{1,0:T(8,128)(2,1)} %wq_hbm.1, bf16[512,128]{1,0:T(8,128)(2,1)} %wk_hbm.1, bf16[512,128]{1,0:T(8,128)(2,1)} %wv_hbm.1, bf16[1024]{0:T(1024)(128)(2,1)} %bq_hbm.1, bf16[128]{0:T(256)(128)(2,1)} %bk_hbm.1, bf16[128]{0:T(256)(128)(2,1)} %bv_hbm.1, ...), custom_call_target="tpu_custom_call" | custom-call | tf_op jit(solution)/shard_map/decode/pallas_call | solution.py:352
  45.3 0.6 %copy.14 = bf16[64,512]{1,0:T(8,128)(2,1)} copy(bf16[64,512]{1,0:T(8,128)(2,1)S(1)} %decode.1) | data formatting | bytes 131072
